TPU v7x, 32 devices: a whole 2x2x4 slice. The times are simulated.
32 devices in a mesh: group: 2 (over y), tensor: 8 (over z, x), seq: 2 (over core).
Axes of the slice: x: 2, y: 2, z: 4, core: 2. Of those that a mesh axis runs over, the one named last changes fastest.
Arguments:
- tokens: bfloat16 [512, 8192], P(('group', 'seq'), 'tensor'), parts along dimension 0, may hold values from -6 to 6
- gate_tiles: bfloat16 [768, 128, 128], P(('tensor', 'seq')), may hold values from -0.09375 to 0.09375
- up_tiles: bfloat16 [768, 128, 128], P(('tensor', 'seq')), may hold values from -0.09375 to 0.09375
- down_tiles: bfloat16 [768, 128, 128], P(('tensor', 'seq')), may hold values from -0.1875 to 0.1875
- in_mask: int32 [16, 64], P('tensor'), may hold values from 0 to 1, as said below
- out_mask: int32 [16, 64], P('tensor'), may hold values from 0 to 1, as said below
- owner_core: int32 [512], P('group'), parts along dimension 0, may hold values from 0 to 1, as said below
Outputs:
- owned: bfloat16 [768, 8192], P(('group', 'seq'), 'tensor'), parts along dimension 0
There are 2 independent parts, one for each index of `group`. A program takes and returns all parts, laid end to end along the dimension named above; an argument that names none is the same for every part. Nothing has to cross between parts.
Inputs may be any that keep to these rules, and one draw needn't show every extreme that they name: `in_mask`: in each group of 2 consecutive rows (the hidden blocks of one tensor index) at most 96 entries are 1, and some group holds exactly 96. `out_mask`: in each group of 2 consecutive rows at most 96 entries are 1, and some group holds exactly 96. `owner_core`: one core owns exactly 192 tokens, forming one run of the cyclic token order; the other core owns the rest.
All inputs are finite; a program needn't handle non-finite values.
Results may differ from a plain program's by a relative error of at most 0.0049.
Values may be sent and summed in bfloat16 or wider, within the bound.
A program may use at most 128 MiB of HBM per device.

v0:
```python
import jax
import jax.numpy as jnp
from jax import lax
from jax.sharding import PartitionSpec as P

CAP = 96
OWN_CAP = 192


def slot_table(mask_rows, capacity):
    hidden_blocks, width_blocks = mask_rows.shape
    flat_mask = mask_rows.reshape(-1)
    rank_of = jnp.cumsum(flat_mask) - 1
    entries = jnp.arange(hidden_blocks * width_blocks, dtype=jnp.int32)
    slot_ids = jnp.arange(capacity, dtype=jnp.int32)
    matched = ((flat_mask[:, None] == 1) & (rank_of[:, None] == slot_ids[None, :])).astype(
        jnp.int32
    )
    live_flag = jnp.sum(matched, axis=0)
    width_index = jnp.sum(matched * (entries % width_blocks)[:, None], axis=0)
    hidden_index = jnp.sum(matched * (entries // width_blocks)[:, None], axis=0)
    return (width_index, hidden_index, live_flag)


def place_input(tiles, width_index, hidden_index, live_flag, width_blocks, hidden_blocks):
    block_size = tiles.shape[1]
    weighted = tiles * live_flag[:, None, None].astype(tiles.dtype)
    grid_tiles = jnp.zeros((width_blocks, hidden_blocks, block_size, block_size), tiles.dtype)
    grid_tiles = grid_tiles.at[width_index, hidden_index].add(weighted)
    return grid_tiles.transpose(0, 2, 1, 3).reshape(
        width_blocks * block_size, hidden_blocks * block_size
    )


def place_output(tiles, width_index, hidden_index, live_flag, width_blocks, hidden_blocks):
    block_size = tiles.shape[1]
    weighted = tiles * live_flag[:, None, None].astype(tiles.dtype)
    grid_tiles = jnp.zeros((hidden_blocks, width_blocks, block_size, block_size), tiles.dtype)
    grid_tiles = grid_tiles.at[hidden_index, width_index].add(weighted)
    return grid_tiles.transpose(0, 2, 1, 3).reshape(
        hidden_blocks * block_size, width_blocks * block_size
    )


def on_device(tokens, gate_tiles, up_tiles, down_tiles, in_mask, out_mask, owner_core):
    row_count = tokens.shape[0]
    hidden_blocks, width_blocks = in_mask.shape
    core_index = lax.axis_index("seq")
    n_cores = lax.axis_size("seq")
    features = lax.all_gather(tokens, "tensor", axis=1, tiled=True)
    width_in, hidden_in, live_in = slot_table(in_mask, CAP)
    width_out, hidden_out, live_out = slot_table(out_mask, CAP)
    gate_all, up_all, down_all = (
        lax.all_gather(gate_tiles, "seq", axis=0, tiled=True),
        lax.all_gather(up_tiles, "seq", axis=0, tiled=True),
        lax.all_gather(down_tiles, "seq", axis=0, tiled=True),
    )
    w_gate = place_input(gate_all, width_in, hidden_in, live_in, width_blocks, hidden_blocks)
    w_up = place_input(up_all, width_in, hidden_in, live_in, width_blocks, hidden_blocks)
    gate_sum = jnp.dot(features, w_gate, preferred_element_type=jnp.float32)
    up_sum = jnp.dot(features, w_up, preferred_element_type=jnp.float32)
    hidden = (jax.nn.silu(gate_sum) * up_sum).astype(jnp.bfloat16)
    w_down = place_output(down_all, width_out, hidden_out, live_out, width_blocks, hidden_blocks)
    partial_value = jnp.dot(hidden, w_down, preferred_element_type=jnp.float32)
    mixed_rows = lax.psum_scatter(partial_value, "tensor", scatter_dimension=1, tiled=True).astype(
        jnp.bfloat16
    )
    core_ids = jnp.arange(n_cores, dtype=jnp.int32)
    row_ids = jnp.arange(row_count, dtype=jnp.int32)
    local_owner = lax.dynamic_slice_in_dim(owner_core, core_index * row_count, row_count, 0)
    owned_flag = (local_owner[None, :] == core_ids[:, None]).astype(jnp.int32)
    order_in = jnp.cumsum(owned_flag, axis=1) - 1
    packing = (
        (owned_flag[:, None, :] == 1) & (order_in[:, None, :] == row_ids[None, :, None])
    ).astype(jnp.bfloat16)
    outgoing = jnp.einsum(
        "dji,ic->djc", packing, mixed_rows, preferred_element_type=jnp.float32
    ).astype(jnp.bfloat16)
    incoming = lax.all_to_all(outgoing, "seq", split_axis=0, concat_axis=0, tiled=True)
    from_each = jnp.sum(
        (owner_core.reshape(n_cores, row_count) == core_index).astype(jnp.int32), axis=1
    )
    offsets = jnp.cumsum(from_each) - from_each
    target_rows = offsets[:, None] + row_ids[None, :]
    valid_rows = row_ids[None, :] < from_each[:, None]
    out_ids = jnp.arange(OWN_CAP, dtype=jnp.int32)
    placing = ((target_rows[None, :, :] == out_ids[:, None, None]) & valid_rows[None, :, :]).astype(
        jnp.bfloat16
    )
    return jnp.einsum("jsi,sic->jc", placing, incoming, preferred_element_type=jnp.float32).astype(
        jnp.bfloat16
    )


def solution(mesh):
    return jax.shard_map(
        on_device,
        mesh=mesh,
        in_specs=(
            P(("group", "seq"), "tensor"),
            P(("tensor", "seq"), None, None),
            P(("tensor", "seq"), None, None),
            P(("tensor", "seq"), None, None),
            P("tensor", None),
            P("tensor", None),
            P("group"),
        ),
        out_specs=P(("group", "seq"), "tensor"),
        check_vma=False,
    )
```

profile of v0, /device:TPU:1, one launch (start us, length us, event | category | flops | bytes accessed | tf_op | source)
XLA Modules:
  0.0 254.7 jit_solution(13570008925765128900)
XLA Ops:
  6.5 0.7 all-gather.5.cloned.1.call-update
  7.3 0.7 all-gather.9.cloned.1.call-update
  8.1 0.7 all-gather.11.cloned.1.call-update
  8.8 0.5 all-gather.7.cloned.1.call-update
  9.4 0.1 reshape.297
  9.5 0.1 reshape.298
  9.7 0.2 reduce-window.25
  9.8 0.2 reduce-window.26
  10.3 0.2 convert_reduce_fusion.1
  10.6 13.0 %all-gather.5.cloned.1.call-done = bf16[96,128,128]{2,1,0:T(8,128)(2,1)} async-done(((bf16[48,128,128]{2,1,0:T(8,128)(2,1)}), bf16[96,128,128]{2,1,0:T(8,128)(2,1)}) %all-gather.5.cloned.1.call-update) | async-done | bytes 3145744 | tf_op jit(solution)/shard_map/all_gather | solution.py:54
  23.5 14.9 %all-gather.9.cloned.1.call-done = bf16[96,128,128]{2,1,0:T(8,128)(2,1)} async-done(((bf16[48,128,128]{2,1,0:T(8,128)(2,1)}), bf16[96,128,128]{2,1,0:T(8,128)(2,1)}) %all-gather.9.cloned.1.call-update) | async-done | bytes 3145744 | tf_op jit(solution)/shard_map/all_gather | solution.py:55
  38.4 5.1 %broadcast_multiply_fusion.2 = (bf16[96,128,128]{2,1,0:T(8,128)(2,1)}, bf16[96,128,128]{2,1,0:T(8,128)(2,1)S(1)}) fusion(bf16[96,128,128]{2,1,0:T(8,128)(2,1)} %all-gather.5.cloned.1.call-done, bf16[96]{0:T(256)(128)(2,1)S(1)} %convert_element_type.58, bf16[96,128,128]{2,1,0:T(8,128)(2,1)} %all-gather.9.cloned.1.call-done), kind=kLoop, calls=%fused_computation.14 | loop fusion | flops 3145728 | bytes 12583104 | tf_op jit(solution)/shard_map/mul | solution.py:27
  43.5 3.0 %broadcast.214.clone.1 = bf16[64,2,128,128]{3,2,1,0:T(8,128)(2,1)} broadcast(bf16[]{:T(256)} %constant.70.clone.1), dimensions={} | broadcast | bytes 4194306 | tf_op jit(solution)/shard_map/broadcast.13
  46.5 21.9 %scatter_fusion = bf16[64,2,128,128]{3,2,1,0:T(8,128)(2,1)} fusion(bf16[64,2,128,128]{3,2,1,0:T(8,128)(2,1)} %broadcast.214.clone.1, s32[96]{0:T(128)S(1)} %fusion.46, bf16[96,128,128]{2,1,0:T(8,128)(2,1)} %get-tuple-element.16), kind=kCustom, calls=%fused_computation | custom fusion | flops 1572864 | bytes 9437952 | tf_op jit(solution)/shard_map/scatter-add | solution.py:29
  68.4 6.6 %copy.21 = bf16[64,128,2,128]{1,0,3,2:T(8,128)(2,1)} copy(bf16[64,128,2,128]{3,1,2,0:T(8,128)(2,1)} %bitcast.81) | data formatting | bytes 8388608 | tf_op jit(solution)/shard_map/transpose | solution.py:30
  75.0 3.0 %broadcast.214.clone = bf16[64,2,128,128]{3,2,1,0:T(8,128)(2,1)} broadcast(bf16[]{:T(256)} %constant.70.clone.1), dimensions={} | broadcast | bytes 4194306 | tf_op jit(solution)/shard_map/broadcast.13
  78.0 20.2 %scatter_fusion.1 = bf16[64,2,128,128]{3,2,1,0:T(8,128)(2,1)} fusion(bf16[64,2,128,128]{3,2,1,0:T(8,128)(2,1)} %broadcast.214.clone, s32[96]{0:T(128)S(1)} %fusion.46, bf16[96,128,128]{2,1,0:T(8,128)(2,1)S(1)} %get-tuple-element.17), kind=kCustom, calls=%fused_computation.1 | custom fusion | flops 1572864 | bytes 9437952 | tf_op jit(solution)/shard_map/scatter-add | solution.py:29
  98.3 6.6 %copy.22 = bf16[64,128,2,128]{1,0,3,2:T(8,128)(2,1)} copy(bf16[64,128,2,128]{3,1,2,0:T(8,128)(2,1)} %bitcast.80) | data formatting | bytes 8388608 | tf_op jit(solution)/shard_map/transpose | solution.py:30
  104.8 2.2 broadcast_multiply_fusion
  107.0 3.0 %broadcast_in_dim.2 = bf16[2,64,128,128]{3,2,1,0:T(8,128)(2,1)} broadcast(bf16[]{:T(256)} %constant.70.clone.1), dimensions={} | broadcast | bytes 4194306 | tf_op jit(solution)/shard_map/broadcast_in_dim | solution.py:38
  110.0 19.4 %scatter_fusion.2 = bf16[2,64,128,128]{3,2,1,0:T(8,128)(2,1)} fusion(bf16[2,64,128,128]{3,2,1,0:T(8,128)(2,1)} %broadcast_in_dim.2, s32[96]{0:T(128)S(1)} %fusion.47, bf16[96,128,128]{2,1,0:T(8,128)(2,1)S(1)} %broadcast_multiply_fusion), kind=kCustom, calls=%fused_computation.2 | custom fusion | flops 1572864 | bytes 9437952 | tf_op jit(solution)/shard_map/scatter-add | solution.py:39
  129.4 6.9 %copy.24 = bf16[2,128,64,128]{3,2,1,0:T(8,128)(2,1)} copy(bf16[2,128,64,128]{3,1,2,0:T(8,128)(2,1)} %bitcast.79) | data formatting | bytes 8388608 | tf_op jit(solution)/shard_map/transpose | solution.py:40
  136.3 5.6 %fusion.10 = f32[128,256]{0,1:T(8,128)S(1)} fusion(bf16[128,8192]{1,0:T(8,128)(2,1)} %all-gather.7.cloned.1.call-done, bf16[32,8,64,128]{3,2,1,0:T(8,128)(2,1)} %bitcast.84), kind=kOutput, calls=%fused_computation.18 | convolution fusion | flops 536870912 | bytes 6422528 | tf_op jit(solution)/shard_map/dot_general | solution.py:60
  141.8 12.9 %fusion = f32[128,8192]{1,0:T(8,128)} fusion(bf16[32,8,64,128]{3,2,1,0:T(8,128)(2,1)} %bitcast.83, bf16[128,8192]{1,0:T(8,128)(2,1)S(1)} %copy-done, bf16[32,8,64,128]{3,2,1,0:T(8,128)(2,1)} %bitcast.82, f32[128,256]{0,1:T(8,128)S(1)} %fusion.10), kind=kOutput, calls=%fused_computation.3 | convolution fusion | flops 1073938432 | bytes 14811136 | tf_op jit(solution)/shard_map/dot_general | solution.py:64
  154.7 0.6 copy-done.3
  155.5 0.3 reduce_window_sum.27
  155.8 0.1 fusion.43
  155.9 0.2 reduce-window.24
  156.2 85.2 %reduce-scatter.2.cloned.1.call-done = f32[128,1024]{1,0:T(8,128)} async-done(((f32[128,8192]{1,0:T(8,128)}), f32[128,1024]{1,0:T(8,128)}) %reduce-scatter.2.cloned.1.call-update) | async-done | bytes 524304 | tf_op jit(solution)/shard_map/reduce_scatter | solution.py:65
  241.4 1.3 convolution_convert_fusion
  242.7 4.4 %all_to_all.5 = bf16[2,128,1024]{2,1,0:T(8,128)(2,1)S(1)} all-to-all(bf16[2,128,1024]{2,1,0:T(8,128)(2,1)S(1)} %convolution_convert_fusion), channel_id=1, replica_groups=mesh['group'=2,'tensor'=8,'seq'=2] {'seq'}, dimensions={0} | all-to-all | bytes 1048576 | tf_op jit(solution)/shard_map/all_to_all | solution.py:79
  247.2 1.0 fusion.9
  (31 shorter events, 0.7 us)
Async XLA Ops:
  6.5 2.8 %copy-start.1 = (s32[2,64]{1,0:T(2,128)S(1)}, s32[2,64]{1,0:T(2,128)}, u32[]{:S(2)}) copy-start(s32[2,64]{1,0:T(2,128)} %param.11) | copy-start | bytes 1540
  6.5 3.0 %copy-start.2 = (s32[2,64]{1,0:T(2,128)S(1)}, s32[2,64]{1,0:T(2,128)}, u32[]{:S(2)}) copy-start(s32[2,64]{1,0:T(2,128)} %param.12) | copy-start | bytes 1540
  6.5 17.0 %all-gather.5.cloned.1.call-start = ((), (), s32[]{:S(2)}) async-start(), calls=%async_computation.2 | async-start | bytes 4718592 | tf_op jit(solution)/shard_map/all_gather | solution.py:54
  7.3 31.1 %all-gather.9.cloned.1.call-start = ((), (), s32[]{:S(2)}) async-start(), calls=%async_computation.4 | async-start | bytes 4718592 | tf_op jit(solution)/shard_map/all_gather | solution.py:55
  8.0 96.8 %all-gather.11.cloned.1.call-start = ((), (), s32[]{:S(2)}) async-start(), calls=%async_computation.5 | async-start | bytes 4718592 | tf_op jit(solution)/shard_map/all_gather | solution.py:56
  8.7 127.5 %all-gather.7.cloned.1.call-start = ((), (), s32[]{:S(2)}) async-start(), calls=%async_computation.3 | async-start | bytes 2359296 | tf_op jit(solution)/shard_map/all_gather | solution.py:50
  9.3 232.1 %reduce-scatter.2.cloned.1.call-start = ((), (), s32[]{:S(2)}) async-start(), calls=%async_computation.6 | async-start | bytes 4718592 | tf_op jit(solution)/shard_map/reduce_scatter | solution.py:65
  136.3 5.6 %copy-start = (bf16[128,8192]{1,0:T(8,128)(2,1)S(1)}, bf16[128,8192]{1,0:T(8,128)(2,1)}, u32[]{:S(2)}) copy-start(bf16[128,8192]{1,0:T(8,128)(2,1)} %all-gather.7.cloned.1.call-done) | copy-start | bytes 6291460
  154.7 0.7 copy-start.3
Sparse Core Ops, SparseCore 0:
  8.9 14.5 all-gather.4
  25.1 13.2 all-gather.8
  39.9 13.2 all-gather.10
  55.3 48.9 all-gather.6
  154.8 86.5 reduce-scatter.1
where the time goes:
time: 257 us; the launch traced here: 255 us
  waiting for transfers between devices  116 us (45%)
  other arithmetic  70.2 us (27%)
  local copies, waits for them, and re-layouts  30.2 us (12%)
  matrix products  20.8 us (8%)
  between operations  13.3 us (5%)
  blocking collectives  4.41 us (2%)
    reduce_scatter x1, waiting for transfers between devices, on_device(): lax.psum_scatter(partial_value, 'tensor', scatter_dimension=1, tiled=True)  85.2 us
    scatter-add x2, other arithmetic, place_input(): grid_tiles = grid_tiles.at[width_index, hidden_index].add(weighted)  42.2 us
    scatter-add x1, other arithmetic, place_output(): grid_tiles = grid_tiles.at[hidden_index, width_index].add(weighted)  19.4 us
    all_gather x1, waiting for transfers between devices, on_device(): lax.all_gather(up_tiles, 'seq', axis=0, tiled=True)  14.9 us
    transpose x2, local copies, waits for them, and re-layouts, place_input(): grid_tiles.transpose(0, 2, 1, 3)  13.2 us
    all_gather x1, waiting for transfers between devices, on_device(): lax.all_gather(gate_tiles, 'seq', axis=0, tiled=True)  13 us
    dot_general x1, matrix products, on_device(): partial_value = jnp.dot(hidden, w_down, preferred_element_type=jnp.float32)  12.9 us
    transpose x1, local copies, waits for them, and re-layouts, place_output(): grid_tiles.transpose(0, 2, 1, 3)  6.86 us
  transfers between devices with their start and end apart: 5, of which 3 were waited for; matrix products, arithmetic and copies ran while one was open for 39% of the time, Pallas kernels for 0%

commit v1 on v0

--- a/solution.py
+++ b/solution.py
@@ -1,10 +1,460 @@
+import functools
+
 import jax
 import jax.numpy as jnp
 from jax import lax
+from jax.experimental import pallas as pl
+from jax.experimental.pallas import tpu as pltpu
 from jax.sharding import PartitionSpec as P
 
 CAP = 96
 OWN_CAP = 192
+MESH = pl.DeviceIdType.MESH
+
+
+def grid_of(n_tensor):
+    n_x = 1 << ((n_tensor.bit_length() - 1) // 2)
+    return n_tensor // n_x, n_x
+
+
+def less(a, b, n):
+    return lax.div(b - a + n, n + 1)
+
+
+def by_distance(z, j, n_z):
+    flip = less(n_z - 1 - z, z, n_z)
+    near = z + flip * (n_z - 1 - 2 * z)
+    k = lax.div(j + 1, 2)
+    both = z + k * (1 - 2 * lax.rem(j, 2))
+    one = j + flip * (n_z - 1 - 2 * j)
+    far = less(2 * near, j, 2 * n_z)
+    return both + far * (one - both)
+
+
+def kernel(
+    n_z,
+    tokens,
+    gate_tiles,
+    up_tiles,
+    down_tiles,
+    in_mask,
+    out_mask,
+    owner,
+    out,
+    feats,
+    gates,
+    ups,
+    downs,
+    slots_in,
+    slots_out,
+    acc,
+    hidden,
+    x_out,
+    x_in,
+    z_out,
+    z_in,
+    mixed,
+    tile_local,
+    tile_send,
+    tile_recv,
+    own_copy,
+    feat_recv,
+    own_send,
+    feat_z_send,
+    feat_x_send,
+    sum_x_send,
+    sum_x_recv,
+    sum_z_send,
+    sum_z_recv,
+    mix_sems,
+):
+    t = lax.axis_index("tensor")
+    s = lax.axis_index("seq")
+    z, x = lax.div(t, 2), lax.rem(t, 2)
+    rows, width = tokens.shape
+    half, block = gate_tiles.shape[0], gate_tiles.shape[1]
+    cap = 2 * half
+    n_blocks = in_mask.shape[1]
+    per_part = width // block
+    pair = 2 * block
+
+    def dev(tt, ss=None):
+        return {"tensor": tt, "seq": s if ss is None else ss}
+
+    def at(zz, xx):
+        return zz * 2 + xx
+
+    x_peer = at(z, 1 - x)
+    core_peer = dev(t, 1 - s)
+
+    barrier = pltpu.get_barrier_semaphore()
+
+    def greet(device):
+        pl.semaphore_signal(barrier, inc=1, device_id=device, device_id_type=MESH)
+
+    greet(core_peer)
+    greet(dev(x_peer))
+
+    @pl.when(z > 0)
+    def _():
+        greet(dev(at(z - 1, x)))
+
+    @pl.when(z < n_z - 1)
+    def _():
+        greet(dev(at(z + 1, x)))
+
+    for dst in (gates, ups, downs):
+        dst[cap] = jnp.zeros((block, block), dst.dtype)
+    acc[...] = jnp.zeros_like(acc)
+
+    local = []
+    for i, (src, dst) in enumerate(((gate_tiles, gates), (up_tiles, ups), (down_tiles, downs))):
+        copy = pltpu.make_async_copy(src, dst.at[pl.ds(s * half, half)], tile_local.at[i])
+        local.append(copy)
+    own = pltpu.make_async_copy(tokens, feats.at[t], own_copy)
+    own.start()
+    for copy in local:
+        copy.start()
+
+    @pl.when((z > 0) & (z < n_z - 1))
+    def _():
+        pl.semaphore_wait(barrier, 4)
+
+    @pl.when((z == 0) | (z == n_z - 1))
+    def _():
+        pl.semaphore_wait(barrier, 3)
+
+    def send(src, dst, send_sem, recv_sem, device):
+        return pltpu.make_async_remote_copy(
+            src_ref=src,
+            dst_ref=dst,
+            send_sem=send_sem,
+            recv_sem=recv_sem,
+            device_id=device,
+            device_id_type=MESH,
+        )
+
+    def own_to(zz, k):
+        return send(tokens, feats.at[t], own_send.at[k], feat_recv.at[t], dev(at(zz, x)))
+
+    own_x = send(tokens, feats.at[t], own_send.at[2], feat_recv.at[t], dev(x_peer))
+    own_x.start()
+
+    @pl.when(z > 0)
+    def _():
+        own_to(z - 1, 0).start()
+
+    @pl.when(z < n_z - 1)
+    def _():
+        own_to(z + 1, 1).start()
+
+    remote = []
+    for i, (src, dst) in enumerate(((gate_tiles, gates), (up_tiles, ups), (down_tiles, downs))):
+        copy = send(
+            src, dst.at[pl.ds(s * half, half)], tile_send.at[i], tile_recv.at[i], core_peer
+        )
+        copy.start()
+        remote.append(copy)
+
+    for mask, table in ((in_mask, slots_in), (out_mask, slots_out)):
+        for c in range(2):
+
+            def fill(b, count, c=c, mask=mask, table=table):
+                bit = mask[c, b]
+                table[c, b] = jnp.where(bit == 1, count, cap)
+                return count + bit
+
+            total = lax.fori_loop(0, n_blocks, fill, jnp.int32(0) if c == 0 else total)
+
+    for i in range(2):
+        local[i].wait()
+        remote[i].wait_recv()
+    own.wait()
+
+    def project(part):
+        def step(i, carry):
+            b = part * per_part + 2 * i
+            a = feats[part, :, pl.ds(pl.multiple_of(i * pair, pair), pair)]
+            for m, tiles in enumerate((gates, ups)):
+                cols = [
+                    jnp.concatenate(
+                        [tiles[slots_in[c, b]], tiles[slots_in[c, b + 1]]], axis=0
+                    )
+                    for c in range(2)
+                ]
+                w = jnp.concatenate(cols, axis=1)
+                acc[m] += jnp.dot(a, w, preferred_element_type=jnp.float32)
+            return carry
+
+        lax.fori_loop(0, per_part // 2, step, 0)
+
+    def arrived(part):
+        send(
+            feats.at[part], feats.at[part], own_send.at[2], feat_recv.at[part], dev(x_peer)
+        ).wait_recv()
+
+    def forward_x(src):
+        part = at(src, x)
+        return send(
+            feats.at[part], feats.at[part], feat_x_send.at[src], feat_recv.at[part], dev(x_peer)
+        )
+
+    def forward_z(src):
+        part = at(src, x)
+        to = z - 1 + 2 * less(src, z, n_z)
+        return send(
+            feats.at[part], feats.at[part], feat_z_send.at[src], feat_recv.at[part],
+            dev(at(to, x)),
+        )
+
+    def goes_on(src):
+        return ((src < z) & (z < n_z - 1)) | ((src > z) & (z > 0))
+
+    project(t)
+
+    def gather_step(j, carry):
+        src = by_distance(z, j, n_z)
+        arrived(at(src, x))
+
+        @pl.when(goes_on(src))
+        def _():
+            forward_z(src).start()
+
+        forward_x(src).start()
+        before = at(by_distance(z, j - 1, n_z), 1 - x)
+        project(at(src, x))
+        arrived(before)
+        project(before)
+        return carry
+
+    lax.fori_loop(1, n_z, gather_step, 0)
+    last = at(by_distance(z, n_z - 1, n_z), 1 - x)
+    arrived(last)
+    project(last)
+
+    gate = acc[0]
+    hidden[...] = (gate / (1.0 + jnp.exp(-gate)) * acc[1]).astype(hidden.dtype)
+
+    local[2].wait()
+    remote[2].wait_recv()
+
+    def down(part, i):
+        b = part * per_part + 2 * i
+        cols = [
+            jnp.concatenate(
+                [downs[slots_out[0, b + k]], downs[slots_out[1, b + k]]], axis=0
+            )
+            for k in range(2)
+        ]
+        w = jnp.concatenate(cols, axis=1)
+        return jnp.dot(hidden[...], w, preferred_element_type=jnp.float32)
+
+    def lanes(i):
+        return pl.ds(pl.multiple_of(i * pair, pair), pair)
+
+    def to_x(dst):
+        return send(
+            x_out.at[dst], x_in.at[dst], sum_x_send.at[dst], sum_x_recv.at[dst], dev(x_peer)
+        )
+
+    def send_x(j, carry):
+        dst = by_distance(z, n_z - 1 - j, n_z)
+
+        def step(i, carry):
+            x_out[dst, :, lanes(i)] = down(at(dst, 1 - x), i).astype(x_out.dtype)
+            return carry
+
+        lax.fori_loop(0, per_part // 2, step, 0)
+        to_x(dst).start()
+        return carry
+
+    lax.fori_loop(0, n_z, send_x, 0)
+
+    def to_z(dst):
+        up = less(z, dst, n_z)
+        return send(
+            z_out.at[dst], z_in.at[dst, 1 - up], sum_z_send.at[dst], sum_z_recv.at[dst, 1 - up],
+            dev(at(z - 1 + 2 * up, x)),
+        )
+
+    def from_z(dst, k):
+        return send(
+            z_out.at[dst], z_in.at[dst, k], sum_z_send.at[dst], sum_z_recv.at[dst, k],
+            dev(x_peer),
+        )
+
+    def partial_sum(dst, i):
+        return down(at(dst, x), i) + x_in[dst, :, lanes(i)].astype(jnp.float32)
+
+    def pass_on(j, carry):
+        dst = by_distance(z, n_z - 1 - j, n_z)
+        side = 1 - less(z, dst, n_z)
+        more = ((dst > z) & (z > 0)) | ((dst < z) & (z < n_z - 1))
+        to_x(dst).wait_recv()
+
+        @pl.when(more)
+        def _():
+            from_z(dst, side).wait_recv()
+
+            def step(i, carry):
+                value = partial_sum(dst, i) + z_in[dst, side, :, lanes(i)].astype(jnp.float32)
+                z_out[dst, :, lanes(i)] = value.astype(z_out.dtype)
+                return carry
+
+            lax.fori_loop(0, per_part // 2, step, 0)
+
+        @pl.when(jnp.logical_not(more))
+        def _():
+            def step(i, carry):
+                z_out[dst, :, lanes(i)] = partial_sum(dst, i).astype(z_out.dtype)
+                return carry
+
+            lax.fori_loop(0, per_part // 2, step, 0)
+
+        to_z(dst).start()
+        return carry
+
+    lax.fori_loop(0, n_z - 1, pass_on, 0)
+
+    to_x(z).wait_recv()
+    side_rows = pl.ds(pl.multiple_of(s * rows, rows), rows)
+
+    @pl.when(z > 0)
+    def _():
+        from_z(z, 0).wait_recv()
+
+    @pl.when(z < n_z - 1)
+    def _():
+        from_z(z, 1).wait_recv()
+
+    def finish(use_below, use_above):
+        def step(i, carry):
+            value = partial_sum(z, i)
+            if use_below:
+                value += z_in[z, 0, :, lanes(i)].astype(jnp.float32)
+            if use_above:
+                value += z_in[z, 1, :, lanes(i)].astype(jnp.float32)
+            mixed[side_rows, lanes(i)] = value.astype(mixed.dtype)
+            return carry
+
+        lax.fori_loop(0, per_part // 2, step, 0)
+
+    @pl.when((z > 0) & (z < n_z - 1))
+    def _():
+        finish(True, True)
+
+    @pl.when(z == 0)
+    def _():
+        finish(False, True)
+
+    @pl.when(z == n_z - 1)
+    def _():
+        finish(True, False)
+
+    swap = send(mixed.at[side_rows], mixed.at[side_rows], mix_sems.at[0], mix_sems.at[1], core_peer)
+    swap.start()
+
+    tokens_all = owner.shape[1]
+    flags = (owner[...] == s).astype(jnp.float32)
+    before = lax.broadcasted_iota(jnp.int32, (tokens_all, tokens_all), 0)
+    after = lax.broadcasted_iota(jnp.int32, (tokens_all, tokens_all), 1)
+    upto = (before <= after).astype(jnp.bfloat16)
+    ranks = jnp.dot(
+        jnp.broadcast_to(flags, (8, tokens_all)).astype(jnp.bfloat16),
+        upto,
+        preferred_element_type=jnp.float32,
+    )[0:1]
+    places = lax.broadcasted_iota(jnp.int32, (out.shape[0], tokens_all), 0).astype(jnp.float32)
+    placing = jnp.where(places + 1.0 == ranks, flags, 0.0).astype(jnp.bfloat16)
+
+    swap.wait_recv()
+
+    def place(i, carry):
+        out[:, lanes(i)] = jnp.dot(
+            placing, mixed[:, lanes(i)], preferred_element_type=jnp.float32
+        ).astype(out.dtype)
+        return carry
+
+    lax.fori_loop(0, per_part // 2, place, 0)
+
+    swap.wait_send()
+    own_x.wait_send()
+
+    @pl.when(z > 0)
+    def _():
+        own_to(z - 1, 0).wait_send()
+
+    @pl.when(z < n_z - 1)
+    def _():
+        own_to(z + 1, 1).wait_send()
+
+    for copy in remote:
+        copy.wait_send()
+
+    def drain(j, carry):
+        other = by_distance(z, j, n_z)
+
+        @pl.when(goes_on(other))
+        def _():
+            forward_z(other).wait_send()
+
+        forward_x(other).wait_send()
+        to_x(other).wait_send()
+        to_z(other).wait_send()
+        return carry
+
+    lax.fori_loop(1, n_z, drain, 0)
+    to_x(z).wait_send()
+
+
+def fused(n_tensor, tokens, gate_tiles, up_tiles, down_tiles, in_mask, out_mask, owner_core):
+    rows, width = tokens.shape
+    half, block, _ = gate_tiles.shape
+    n_z, n_x = grid_of(n_tensor)
+    cap = 2 * half
+    n_hidden = in_mask.shape[0] * block
+    kind = tokens.dtype
+    everywhere = pl.BlockSpec(memory_space=pl.ANY)
+    scalars = pl.BlockSpec(memory_space=pltpu.SMEM)
+    vmem = pl.BlockSpec(memory_space=pltpu.VMEM)
+    dma = pltpu.SemaphoreType.DMA
+    return pl.pallas_call(
+        functools.partial(kernel, n_z),
+        out_shape=jax.ShapeDtypeStruct((OWN_CAP, width), kind),
+        in_specs=[everywhere] * 4 + [scalars] * 2 + [vmem],
+        out_specs=vmem,
+        scratch_shapes=[
+            pltpu.VMEM((n_tensor, rows, width), kind),
+            pltpu.VMEM((cap + 1, block, block), kind),
+            pltpu.VMEM((cap + 1, block, block), kind),
+            pltpu.VMEM((cap + 1, block, block), kind),
+            pltpu.SMEM(in_mask.shape, jnp.int32),
+            pltpu.SMEM(out_mask.shape, jnp.int32),
+            pltpu.VMEM((2, rows, n_hidden), jnp.float32),
+            pltpu.VMEM((rows, n_hidden), kind),
+            pltpu.VMEM((n_z, rows, width), kind),
+            pltpu.VMEM((n_z, rows, width), kind),
+            pltpu.VMEM((n_z, rows, width), kind),
+            pltpu.VMEM((n_z, 2, rows, width), kind),
+            pltpu.VMEM((2 * rows, width), kind),
+            dma((3,)),
+            dma((3,)),
+            dma((3,)),
+            dma,
+            dma((n_tensor,)),
+            dma((3,)),
+            dma((n_z,)),
+            dma((n_z,)),
+            dma((n_z,)),
+            dma((n_z,)),
+            dma((n_z,)),
+            dma((n_z, 2)),
+            dma((2,)),
+        ],
+        compiler_params=pltpu.CompilerParams(
+            collective_id=0, has_side_effects=True, vmem_limit_bytes=48 << 20
+        ),
+    )(tokens, gate_tiles, up_tiles, down_tiles, in_mask, out_mask, owner_core[None, :])
 
 
 def slot_table(mask_rows, capacity):
@@ -93,8 +543,16 @@
 
 
 def solution(mesh):
+    n_tensor = mesh.shape["tensor"]
+
+    def step(tokens, gate_tiles, up_tiles, down_tiles, in_mask, out_mask, owner_core):
+        form = on_device
+        if grid_of(n_tensor)[1] == 2 and tokens.shape[1] % (2 * gate_tiles.shape[1]) == 0:
+            form = functools.partial(fused, n_tensor)
+        return form(tokens, gate_tiles, up_tiles, down_tiles, in_mask, out_mask, owner_core)
+
     return jax.shard_map(
-        on_device,
+        step,
         mesh=mesh,
         in_specs=(
             P(("group", "seq"), "tensor"),

time: 257 us -> 77.3 us (0.30)
  the two profiles are of different devices: /device:TPU:1 before, /device:TPU:11 now
where the time goes in v1:
time: 77.3 us; the launch traced here: 77 us
  Pallas kernels  69.1 us (89%)
  local copies, waits for them, and re-layouts  7.96 us (10%)
    pallas_call x1, Pallas kernels, fused(): pl.pallas_call(functools.partial(kernel, n_z), out_shape=jax.ShapeDtypeSt...  69.1 us
    unnamed x15, local copies, waits for them, and re-layouts  7.96 us

profile of v1, /device:TPU:11, one launch (start us, length us, event | category | flops | bytes accessed | tf_op | source)
XLA Modules:
  0.0 77.0 jit_solution(16611139599854719776)
XLA Ops:
  0.0 0.0 copy-start
  0.0 1.4 %copy-done = bf16[48,128,128]{2,1,0:T(8,128)(2,1)S(1)} copy-done((bf16[48,128,128]{2,1,0:T(8,128)(2,1)S(1)}, bf16[48,128,128]{2,1,0:T(8,128)(2,1)}, u32[]{:S(2)}) %copy-start) | copy-done | bytes 1572888
  1.4 0.0 copy-start.1
  1.4 1.4 %copy-done.1 = bf16[48,128,128]{2,1,0:T(8,128)(2,1)S(1)} copy-done((bf16[48,128,128]{2,1,0:T(8,128)(2,1)S(1)}, bf16[48,128,128]{2,1,0:T(8,128)(2,1)}, u32[]{:S(2)}) %copy-start.1) | copy-done | bytes 1572888
  2.8 0.0 copy-start.2
  2.8 1.4 %copy-done.2 = bf16[48,128,128]{2,1,0:T(8,128)(2,1)S(1)} copy-done((bf16[48,128,128]{2,1,0:T(8,128)(2,1)S(1)}, bf16[48,128,128]{2,1,0:T(8,128)(2,1)}, u32[]{:S(2)}) %copy-start.2) | copy-done | bytes 1572888
  4.2 0.0 copy-start.3
  4.2 0.9 %copy-done.3 = bf16[128,1024]{1,0:T(8,128)(2,1)S(1)} copy-done((bf16[128,1024]{1,0:T(8,128)(2,1)S(1)}, bf16[128,1024]{1,0:T(8,128)(2,1)}, u32[]{:S(2)}) %copy-start.3) | copy-done | bytes 262168
  5.2 0.0 copy-start.4
  5.2 0.7 copy-done.4
  5.9 0.0 copy-start.5
  5.9 0.7 copy-done.5
  6.5 0.0 copy-start.6
  6.5 0.7 copy-done.6
  7.2 69.1 %shard_map.73 = bf16[192,1024]{1,0:T(8,128)(2,1)S(1)} custom-call(bf16[128,1024]{1,0:T(8,128)(2,1)S(1)} %copy-done.3, bf16[48,128,128]{2,1,0:T(8,128)(2,1)S(1)} %copy-done, bf16[48,128,128]{2,1,0:T(8,128)(2,1)S(1)} %copy-done.1, bf16[48,128,128]{2,1,0:T(8,128)(2,1)S(1)} %copy-done.2, s32[2,64]{1,0:T(2,128)S(1)} %copy-done.4, s32[2,64]{1,0:T(2,128)S(1)} %copy-done.5, ...), custom_call_target="tpu_custom_call" | custom-call | tf_op jit(solution)/shard_map/pallas_call | solution.py:421
  76.3 0.7 copy.9
Async XLA Ops:
  0.0 1.4 %copy-start = (bf16[48,128,128]{2,1,0:T(8,128)(2,1)S(1)}, bf16[48,128,128]{2,1,0:T(8,128)(2,1)}, u32[]{:S(2)}) copy-start(bf16[48,128,128]{2,1,0:T(8,128)(2,1)} %gate_tiles.1) | copy-start | bytes 4718596
  1.4 1.4 %copy-start.1 = (bf16[48,128,128]{2,1,0:T(8,128)(2,1)S(1)}, bf16[48,128,128]{2,1,0:T(8,128)(2,1)}, u32[]{:S(2)}) copy-start(bf16[48,128,128]{2,1,0:T(8,128)(2,1)} %up_tiles.1) | copy-start | bytes 4718596
  2.8 1.4 %copy-start.2 = (bf16[48,128,128]{2,1,0:T(8,128)(2,1)S(1)}, bf16[48,128,128]{2,1,0:T(8,128)(2,1)}, u32[]{:S(2)}) copy-start(bf16[48,128,128]{2,1,0:T(8,128)(2,1)} %down_tiles.1) | copy-start | bytes 4718596
  4.2 0.9 %copy-start.3 = (bf16[128,1024]{1,0:T(8,128)(2,1)S(1)}, bf16[128,1024]{1,0:T(8,128)(2,1)}, u32[]{:S(2)}) copy-start(bf16[128,1024]{1,0:T(8,128)(2,1)} %tokens.1) | copy-start | bytes 786436
  5.2 0.7 copy-start.4
  5.9 0.7 copy-start.5
  6.5 0.7 copy-start.6

commit v2 on v0

--- a/solution.py
+++ b/solution.py
@@ -1,10 +1,536 @@
+import functools
+
 import jax
 import jax.numpy as jnp
 from jax import lax
+from jax.experimental import pallas as pl
+from jax.experimental.pallas import tpu as pltpu
 from jax.sharding import PartitionSpec as P
 
 CAP = 96
 OWN_CAP = 192
+PIECES = 2
+VMEM_LIMIT = 64 << 20
+MESH = pl.DeviceIdType.MESH
+
+
+def grid_of(n_tensor):
+    n_x = 1 << ((n_tensor.bit_length() - 1) // 2)
+    return n_tensor // n_x, n_x
+
+
+def less(a, b, n):
+    return lax.div(b - a + n, n + 1)
+
+
+def by_distance(z, j, n_z):
+    flip = less(n_z - 1 - z, z, n_z)
+    near = z + flip * (n_z - 1 - 2 * z)
+    k = lax.div(j + 1, 2)
+    both = z + k * (1 - 2 * lax.rem(j, 2))
+    one = j + flip * (n_z - 1 - 2 * j)
+    far = less(2 * near, j, 2 * n_z)
+    return both + far * (one - both)
+
+
+def kernel(
+    n_z,
+    pieces,
+    tokens,
+    gate_tiles,
+    up_tiles,
+    down_tiles,
+    in_mask_hbm,
+    out_mask_hbm,
+    owner_hbm,
+    out,
+    feats,
+    gates,
+    ups,
+    downs,
+    slots_in,
+    slots_out,
+    acc,
+    hidden,
+    x_out,
+    x_in,
+    z_out,
+    z_in,
+    side_out,
+    side_in,
+    mixed,
+    in_mask,
+    out_mask,
+    owner,
+    small_copy,
+    tile_local,
+    tile_send,
+    tile_recv,
+    own_copy,
+    feat_recv,
+    own_send,
+    feat_z_send,
+    feat_x_send,
+    peer_send,
+    sum_x_send,
+    sum_x_recv,
+    sum_z_send,
+    sum_z_recv,
+    side_send,
+    side_recv,
+    mix_send,
+    mix_recv,
+):
+    t = lax.axis_index("tensor")
+    s = lax.axis_index("seq")
+    z, x = lax.div(t, 2), lax.rem(t, 2)
+    rows = tokens.shape[0]
+    span = tokens.shape[1] // pieces
+    half, block = gate_tiles.shape[0], gate_tiles.shape[1]
+    cap = 2 * half
+    n_blocks = in_mask.shape[1]
+    per_piece = span // block
+    pair = 2 * block
+    last = pieces - 1
+    has_below, has_above = z > 0, z < n_z - 1
+
+    def dev(tt, ss=None):
+        return {"tensor": tt, "seq": s if ss is None else ss}
+
+    def at(zz, xx):
+        return zz * 2 + xx
+
+    x_peer = dev(at(z, 1 - x))
+    core_peer = dev(t, 1 - s)
+    below, above = dev(at(z - 1, x)), dev(at(z + 1, x))
+
+    def send(src, dst, send_sem, recv_sem, device):
+        return pltpu.make_async_remote_copy(
+            src_ref=src,
+            dst_ref=dst,
+            send_sem=send_sem,
+            recv_sem=recv_sem,
+            device_id=device,
+            device_id_type=MESH,
+        )
+
+    def when(condition, act):
+        pl.when(condition)(act)
+
+    barrier = pltpu.get_barrier_semaphore()
+
+    def greet(device):
+        pl.semaphore_signal(barrier, inc=1, device_id=device, device_id_type=MESH)
+
+    greet(core_peer)
+    greet(x_peer)
+    when(has_below, lambda: greet(below))
+    when(has_above, lambda: greet(above))
+
+    stacks = ((gate_tiles, gates), (up_tiles, ups), (down_tiles, downs))
+    mine = pl.ds(s * half, half)
+    smalls = ((in_mask_hbm, in_mask), (out_mask_hbm, out_mask), (owner_hbm, owner))
+    small = [pltpu.make_async_copy(*smalls[i], small_copy.at[i]) for i in range(3)]
+    for copy in small:
+        copy.start()
+    own = [
+        pltpu.make_async_copy(
+            tokens.at[:, pl.ds(p * span, span)], feats.at[t * pieces + p], own_copy.at[p]
+        )
+        for p in range(pieces)
+    ]
+    for copy in own:
+        copy.start()
+    local = [
+        pltpu.make_async_copy(src, dst.at[mine], tile_local.at[i])
+        for i, (src, dst) in enumerate(stacks)
+    ]
+    for copy in local:
+        copy.start()
+
+    when(has_below & has_above, lambda: pl.semaphore_wait(barrier, 4))
+    when(jnp.logical_not(has_below & has_above), lambda: pl.semaphore_wait(barrier, 3))
+
+    def own_to(p, k):
+        return send(
+            tokens.at[:, pl.ds(p * span, span)],
+            feats.at[t * pieces + p],
+            own_send.at[k, p],
+            feat_recv.at[t * pieces + p],
+            (x_peer, below, above)[k],
+        )
+
+    for p in range(pieces):
+        own_to(p, 0).start()
+        when(has_below, lambda: own_to(p, 1).start())
+        when(has_above, lambda: own_to(p, 2).start())
+
+    remote = [
+        send(src, dst.at[mine], tile_send.at[i], tile_recv.at[i], core_peer)
+        for i, (src, dst) in enumerate(stacks)
+    ]
+    for copy in remote:
+        copy.start()
+
+    for dst in (gates, ups, downs):
+        dst[cap] = jnp.zeros((block, block), dst.dtype)
+    acc[...] = jnp.zeros_like(acc)
+
+    for copy in small:
+        copy.wait()
+    for mask, table in ((in_mask, slots_in), (out_mask, slots_out)):
+        total = jnp.int32(0)
+        for c in range(2):
+
+            def fill(b, count, c=c, mask=mask, table=table):
+                bit = mask[c, b]
+                table[c, b] = jnp.where(bit == 1, count, cap)
+                return count + bit
+
+            total = lax.fori_loop(0, n_blocks, fill, total)
+
+    for i in range(2):
+        local[i].wait()
+        remote[i].wait_recv()
+
+    def lanes(i):
+        return pl.ds(pl.multiple_of(i * pair, pair), pair)
+
+    def project(part):
+        def step(i, carry):
+            b = part * per_piece + 2 * i
+            a = feats[part, :, lanes(i)]
+            for m, tiles in enumerate((gates, ups)):
+                cols = [
+                    jnp.concatenate([tiles[slots_in[c, b]], tiles[slots_in[c, b + 1]]], axis=0)
+                    for c in range(2)
+                ]
+                w = jnp.concatenate(cols, axis=1)
+                acc[m] += jnp.dot(a, w, preferred_element_type=jnp.float32)
+            return carry
+
+        lax.fori_loop(0, per_piece // 2, step, 0)
+
+    def passed(part, sem, device):
+        return send(feats.at[part], feats.at[part], sem, feat_recv.at[part], device)
+
+    def arrived(part):
+        passed(part, own_send.at[0, 0], x_peer).wait_recv()
+
+    def forward_x(src, p):
+        return passed(at(src, x) * pieces + p, feat_x_send.at[src, p], x_peer)
+
+    def forward_z(src, p):
+        to = z - 1 + 2 * less(src, z, n_z)
+        return passed(at(src, x) * pieces + p, feat_z_send.at[src, p], dev(at(to, x)))
+
+    peer_last = at(z, 1 - x) * pieces + last
+
+    def forward_peer(k):
+        return passed(peer_last, peer_send.at[k], (below, above)[k])
+
+    def goes_on(src):
+        return ((src < z) & has_above) | ((src > z) & has_below)
+
+    def by_x(other, p):
+        near = (other == z - 1) | (other == z + 1)
+        return jnp.logical_not(near & (p == last))
+
+    for p in range(pieces):
+        own[p].wait()
+        project(t * pieces + p)
+    for p in range(pieces):
+        arrived(at(z, 1 - x) * pieces + p)
+        if p == last:
+            when(has_below, lambda: forward_peer(0).start())
+            when(has_above, lambda: forward_peer(1).start())
+
+    def gather_step(k, carry):
+        j, p = lax.div(k, pieces), lax.rem(k, pieces)
+        src = by_distance(z, j, n_z)
+        arrived(at(src, x) * pieces + p)
+        when(goes_on(src), lambda: forward_z(src, p).start())
+        when(by_x(src, p), lambda: forward_x(src, p).start())
+        before = by_distance(z, j - 1, n_z)
+        part = at(before, 1 - x) * pieces + p
+
+        when(j > 1, lambda: arrived(part))
+        project(part)
+        project(at(src, x) * pieces + p)
+        return carry
+
+    lax.fori_loop(pieces, n_z * pieces, gather_step, 0)
+    farthest = at(by_distance(z, n_z - 1, n_z), 1 - x) * pieces
+    for p in range(pieces):
+        arrived(farthest + p)
+        project(farthest + p)
+
+    gate = acc[0]
+    hidden[...] = (gate / (1.0 + jnp.exp(-gate)) * acc[1]).astype(hidden.dtype)
+
+    local[2].wait()
+    remote[2].wait_recv()
+
+    def down(part, i):
+        b = part * per_piece + 2 * i
+        cols = [
+            jnp.concatenate([downs[slots_out[0, b + k]], downs[slots_out[1, b + k]]], axis=0)
+            for k in range(2)
+        ]
+        w = jnp.concatenate(cols, axis=1)
+        return jnp.dot(hidden[...], w, preferred_element_type=jnp.float32)
+
+    def each(store):
+        def step(i, carry):
+            store(i)
+            return carry
+
+        lax.fori_loop(0, per_piece // 2, step, 0)
+
+    def wide(value):
+        return value.astype(jnp.float32)
+
+    def side_to(k):
+        return send(
+            side_out.at[k], side_in.at[1 - k], side_send.at[k], side_recv.at[1 - k],
+            (below, above)[k],
+        )
+
+    def side_go(k):
+        dst = z - 1 + 2 * k
+
+        def store(i):
+            part = at(dst, 1 - x) * pieces + last
+            side_out[k, :, lanes(i)] = down(part, i).astype(side_out.dtype)
+
+        each(store)
+        side_to(k).start()
+
+    def to_x(dst, p):
+        return send(
+            x_out.at[dst, p], x_in.at[dst, p], sum_x_send.at[dst, p], sum_x_recv.at[dst, p], x_peer
+        )
+
+    def go_x(dst, p):
+        def store(i):
+            value = down(at(dst, 1 - x) * pieces + p, i)
+            x_out[dst, p, :, lanes(i)] = value.astype(x_out.dtype)
+
+        each(store)
+        to_x(dst, p).start()
+
+    def send_x(k, carry):
+        j, p = n_z - 1 - lax.div(k, pieces), lax.rem(k, pieces)
+        dst = by_distance(z, j, n_z)
+        when(by_x(dst, p), lambda: go_x(dst, p))
+        return carry
+
+    lax.fori_loop(0, pieces, send_x, 0)
+    when(has_below, lambda: side_go(0))
+    when(has_above, lambda: side_go(1))
+    lax.fori_loop(pieces, n_z * pieces - 1, send_x, 0)
+
+    def go_x_last(use_below, use_above):
+        def store(i):
+            value = down(at(z, 1 - x) * pieces + last, i)
+            if use_below:
+                value += wide(side_in[0, :, lanes(i)])
+            if use_above:
+                value += wide(side_in[1, :, lanes(i)])
+            x_out[z, last, :, lanes(i)] = value.astype(x_out.dtype)
+
+        if use_below:
+            side_from(0)
+        if use_above:
+            side_from(1)
+        each(store)
+        to_x(z, last).start()
+
+    def side_from(k):
+        send(
+            side_out.at[k], side_in.at[k], side_send.at[k], side_recv.at[k], x_peer
+        ).wait_recv()
+
+    def by_place(act):
+        when(has_below & has_above, lambda: act(True, True))
+        when(z == 0, lambda: act(False, True))
+        when(z == n_z - 1, lambda: act(True, False))
+
+    by_place(go_x_last)
+
+    def to_z(dst, p):
+        up = less(z, dst, n_z)
+        return send(
+            z_out.at[dst, p], z_in.at[dst, 1 - up, p], sum_z_send.at[dst, p],
+            sum_z_recv.at[dst, 1 - up, p], dev(at(z - 1 + 2 * up, x)),
+        )
+
+    def from_z(dst, k, p):
+        send(
+            z_out.at[dst, p], z_in.at[dst, k, p], sum_z_send.at[dst, p],
+            sum_z_recv.at[dst, k, p], x_peer,
+        ).wait_recv()
+
+    def pass_on(k, carry):
+        j, p = n_z - 1 - lax.div(k, pieces), lax.rem(k, pieces)
+        dst = by_distance(z, j, n_z)
+        side = 1 - less(z, dst, n_z)
+        more = ((dst > z) & has_below) | ((dst < z) & has_above)
+        crossed = by_x(dst, p)
+        when(crossed, lambda: to_x(dst, p).wait_recv())
+        when(more, lambda: from_z(dst, side, p))
+
+        def go(use_x, use_z):
+            def store(i):
+                value = down(at(dst, x) * pieces + p, i)
+                if use_x:
+                    value += wide(x_in[dst, p, :, lanes(i)])
+                if use_z:
+                    value += wide(z_in[dst, side, p, :, lanes(i)])
+                z_out[dst, p, :, lanes(i)] = value.astype(z_out.dtype)
+
+            each(store)
+
+        alone = jnp.logical_not(more)
+        when(crossed & more, lambda: go(True, True))
+        when(crossed & alone, lambda: go(True, False))
+        when(jnp.logical_not(crossed) & more, lambda: go(False, True))
+        when(jnp.logical_not(crossed) & alone, lambda: go(False, False))
+        to_z(dst, p).start()
+        return carry
+
+    lax.fori_loop(0, (n_z - 1) * pieces, pass_on, 0)
+
+    mine = pl.ds(pl.multiple_of(s * rows, rows), rows)
+
+    def swap(p):
+        return send(
+            mixed.at[p, mine], mixed.at[p, mine], mix_send.at[p], mix_recv.at[p], core_peer
+        )
+
+    def finish(p, use_below, use_above):
+        def store(i):
+            value = down(t * pieces + p, i) + wide(x_in[z, p, :, lanes(i)])
+            if use_below:
+                value += wide(z_in[z, 0, p, :, lanes(i)])
+            if use_above:
+                value += wide(z_in[z, 1, p, :, lanes(i)])
+            mixed[p, mine, lanes(i)] = value.astype(mixed.dtype)
+
+        if use_below:
+            from_z(z, 0, p)
+        if use_above:
+            from_z(z, 1, p)
+        each(store)
+
+    tokens_all = owner.shape[1]
+    flags = (owner[...] == s).astype(jnp.float32)
+    first = lax.broadcasted_iota(jnp.int32, (tokens_all, tokens_all), 0)
+    second = lax.broadcasted_iota(jnp.int32, (tokens_all, tokens_all), 1)
+    upto = (first <= second).astype(jnp.bfloat16)
+    ranks = jnp.dot(
+        jnp.broadcast_to(flags, (8, tokens_all)).astype(jnp.bfloat16),
+        upto,
+        preferred_element_type=jnp.float32,
+    )[0:1]
+    places = lax.broadcasted_iota(jnp.int32, (out.shape[0], tokens_all), 0).astype(jnp.float32)
+    placing = jnp.where(places + 1.0 == ranks, flags, 0.0).astype(jnp.bfloat16)
+
+    for p in range(pieces):
+        to_x(z, p).wait_recv()
+        by_place(functools.partial(finish, p))
+        swap(p).start()
+
+    for p in range(pieces):
+        swap(p).wait_recv()
+        for i in range(per_piece // 2):
+            out[:, pl.ds(p * span + i * pair, pair)] = jnp.dot(
+                placing, mixed[p, :, pl.ds(i * pair, pair)], preferred_element_type=jnp.float32
+            ).astype(out.dtype)
+
+    for p in range(pieces):
+        swap(p).wait_send()
+        own_to(p, 0).wait_send()
+        when(has_below, lambda: own_to(p, 1).wait_send())
+        when(has_above, lambda: own_to(p, 2).wait_send())
+        to_x(z, p).wait_send()
+    for k, there in enumerate((has_below, has_above)):
+        when(there, lambda: forward_peer(k).wait_send())
+        when(there, lambda: side_to(k).wait_send())
+    for copy in remote:
+        copy.wait_send()
+
+    def drain(k, carry):
+        j, p = lax.div(k, pieces), lax.rem(k, pieces)
+        other = by_distance(z, j, n_z)
+        when(goes_on(other), lambda: forward_z(other, p).wait_send())
+        when(by_x(other, p), lambda: forward_x(other, p).wait_send())
+        when(by_x(other, p), lambda: to_x(other, p).wait_send())
+        to_z(other, p).wait_send()
+        return carry
+
+    lax.fori_loop(pieces, n_z * pieces, drain, 0)
+
+
+def fused(n_tensor, tokens, gate_tiles, up_tiles, down_tiles, in_mask, out_mask, owner_core):
+    rows, width = tokens.shape
+    half, block, _ = gate_tiles.shape
+    n_z, n_x = grid_of(n_tensor)
+    pieces = PIECES
+    span = width // pieces
+    cap = 2 * half
+    n_hidden = in_mask.shape[0] * block
+    kind = tokens.dtype
+    hbm = pl.BlockSpec(memory_space=pltpu.HBM)
+    vmem = pl.BlockSpec(memory_space=pltpu.VMEM)
+    dma = pltpu.SemaphoreType.DMA
+    return pl.pallas_call(
+        functools.partial(kernel, n_z, pieces),
+        out_shape=jax.ShapeDtypeStruct((OWN_CAP, width), kind),
+        in_specs=[hbm] * 7,
+        out_specs=vmem,
+        scratch_shapes=[
+            pltpu.VMEM((n_tensor * pieces, rows, span), kind),
+            pltpu.VMEM((cap + 1, block, block), kind),
+            pltpu.VMEM((cap + 1, block, block), kind),
+            pltpu.VMEM((cap + 1, block, block), kind),
+            pltpu.SMEM(in_mask.shape, jnp.int32),
+            pltpu.SMEM(out_mask.shape, jnp.int32),
+            pltpu.VMEM((2, rows, n_hidden), jnp.float32),
+            pltpu.VMEM((rows, n_hidden), kind),
+            pltpu.VMEM((n_z, pieces, rows, span), kind),
+            pltpu.VMEM((n_z, pieces, rows, span), kind),
+            pltpu.VMEM((n_z, pieces, rows, span), kind),
+            pltpu.VMEM((n_z, 2, pieces, rows, span), kind),
+            pltpu.VMEM((2, rows, span), kind),
+            pltpu.VMEM((2, rows, span), kind),
+            pltpu.VMEM((pieces, 2 * rows, span), kind),
+            pltpu.SMEM(in_mask.shape, jnp.int32),
+            pltpu.SMEM(out_mask.shape, jnp.int32),
+            pltpu.VMEM((1,) + owner_core.shape, jnp.int32),
+            dma((3,)),
+            dma((3,)),
+            dma((3,)),
+            dma((3,)),
+            dma((pieces,)),
+            dma((n_tensor * pieces,)),
+            dma((3, pieces)),
+            dma((n_z, pieces)),
+            dma((n_z, pieces)),
+            dma((2,)),
+            dma((n_z, pieces)),
+            dma((n_z, pieces)),
+            dma((n_z, pieces)),
+            dma((n_z, 2, pieces)),
+            dma((2,)),
+            dma((2,)),
+            dma((pieces,)),
+            dma((pieces,)),
+        ],
+        compiler_params=pltpu.CompilerParams(
+            collective_id=0, has_side_effects=True, vmem_limit_bytes=VMEM_LIMIT
+        ),
+    )(tokens, gate_tiles, up_tiles, down_tiles, in_mask, out_mask, owner_core[None, :])
 
 
 def slot_table(mask_rows, capacity):
@@ -93,8 +619,16 @@
 
 
 def solution(mesh):
+    n_tensor = mesh.shape["tensor"]
+
+    def step(tokens, gate_tiles, up_tiles, down_tiles, in_mask, out_mask, owner_core):
+        form = on_device
+        if grid_of(n_tensor)[1] == 2 and tokens.shape[1] % (2 * PIECES * gate_tiles.shape[1]) == 0:
+            form = functools.partial(fused, n_tensor)
+        return form(tokens, gate_tiles, up_tiles, down_tiles, in_mask, out_mask, owner_core)
+
     return jax.shard_map(
-        on_device,
+        step,
         mesh=mesh,
         in_specs=(
             P(("group", "seq"), "tensor"),

time: 257 us -> 62.4 us (0.24)
  waiting for transfers between devices: 116 us -> 0 us
  other arithmetic: 70.2 us -> 0 us
  Pallas kernels: 0 us -> 60.5 us
  local copies, waits for them, and re-layouts: 30.2 us -> 1.77 us
  matrix products: 20.8 us -> 0 us
  between operations: 13.3 us -> 0.01 us
  blocking collectives: 4.41 us -> 0 us
    reduce_scatter x1 -> x0, waiting for transfers between devices: 85.2 us -> none  [on_device(): lax.psum_scatter(partial_value, 'tensor', scatter_dimension=1, tiled=True)]
    scatter-add x3 -> x0, other arithmetic: 61.5 us -> none  [the longest x2 42.2 us: place_input(): grid_tiles = grid_tiles.at[width_index, hidden_index].add(weighted)]
    pallas_call x0 -> x1, Pallas kernels: none -> 60.5 us  [fused(): pl.pallas_call(functools.partial(kernel, n_z, pieces), out_shape=jax.Shap...]
    all_gather x4 -> x0, waiting for transfers between devices: 27.8 us -> none  [the longest x1 14.9 us: on_device(): lax.all_gather(up_tiles, 'seq', axis=0, tiled=True)]
    dot_general x4 -> x0, matrix products: 20.8 us -> none  [the longest x1 12.9 us: on_device(): partial_value = jnp.dot(hidden, w_down, preferred_element_type=jnp.float32)]
    transpose x3 -> x0, local copies, waits for them, and re-layouts: 20 us -> none  [the longest x2 13.2 us: place_input(): grid_tiles.transpose(0, 2, 1, 3)]
    mul x2 -> x0, other arithmetic: 7.26 us -> none  [the longest x1 5.1 us: place_input(): weighted = tiles * live_flag[:, None, None].astype(tiles.dtype)]
    another operation x4 -> x0, local copies, waits for them, and re-layouts: 6.3 us -> none
  transfers between devices with their start and end apart: 5 -> 0, of which waited for: 3 -> 0; matrix products, arithmetic and copies ran while one was open for 39% -> 0% of each run, Pallas kernels for 0% -> 0%
where the time goes in v2:
time: 62.4 us; the launch traced here: 62.3 us
  Pallas kernels  60.5 us (97%)
  local copies, waits for them, and re-layouts  1.77 us (3%)
    pallas_call x1, Pallas kernels, fused(): pl.pallas_call(functools.partial(kernel, n_z, pieces), out_shape=jax.Shap...  60.5 us
    unnamed x1, local copies, waits for them, and re-layouts  1.77 us

profile of v2, /device:TPU:1, one launch (start us, length us, event | category | flops | bytes accessed | tf_op | source)
XLA Modules:
  0.0 62.3 jit_solution(8057437988482427480)
XLA Ops:
  0.0 60.5 %shard_map.73 = bf16[192,1024]{1,0:T(8,128)(2,1)} custom-call(bf16[128,1024]{1,0:T(8,128)(2,1)} %tokens.1, bf16[48,128,128]{2,1,0:T(8,128)(2,1)} %gate_tiles.1, bf16[48,128,128]{2,1,0:T(8,128)(2,1)} %up_tiles.1, bf16[48,128,128]{2,1,0:T(8,128)(2,1)} %down_tiles.1, s32[2,64]{1,0:T(2,128)} %in_mask_hbm.1, s32[2,64]{1,0:T(2,128)} %out_mask_hbm.1, s32[1,256]{1,0:T(1,128)} %bitcast.1), custom_call_target="tpu_custom_call" | custom-call | tf_op jit(solution)/shard_map/pallas_call | solution.py:487
  60.5 1.8 %copy.9 = bf16[192,1024]{1,0:T(8,128)(2,1)} copy(bf16[192,1024]{1,0:T(8,128)(2,1)} %shard_map.73) | data formatting | bytes 786432

commit v3 on v2

--- a/solution.py
+++ b/solution.py
@@ -10,6 +10,7 @@
 CAP = 96
 OWN_CAP = 192
 PIECES = 2
+SIDE = 1
 VMEM_LIMIT = 64 << 20
 MESH = pl.DeviceIdType.MESH
 
@@ -91,7 +92,7 @@
     n_blocks = in_mask.shape[1]
     per_piece = span // block
     pair = 2 * block
-    last = pieces - 1
+    straight = pieces - SIDE
     has_below, has_above = z > 0, z < n_z - 1
 
     def dev(tt, ss=None):
@@ -153,7 +154,7 @@
 
     def own_to(p, k):
         return send(
-            tokens.at[:, pl.ds(p * span, span)],
+            feats.at[t * pieces + p],
             feats.at[t * pieces + p],
             own_send.at[k, p],
             feat_recv.at[t * pieces + p],
@@ -161,6 +162,7 @@
         )
 
     for p in range(pieces):
+        own[p].wait()
         own_to(p, 0).start()
         when(has_below, lambda: own_to(p, 1).start())
         when(has_above, lambda: own_to(p, 2).start())
@@ -176,22 +178,19 @@
         dst[cap] = jnp.zeros((block, block), dst.dtype)
     acc[...] = jnp.zeros_like(acc)
 
-    for copy in small:
-        copy.wait()
-    for mask, table in ((in_mask, slots_in), (out_mask, slots_out)):
+    def number(mask, table):
         total = jnp.int32(0)
         for c in range(2):
 
-            def fill(b, count, c=c, mask=mask, table=table):
+            def fill(b, count, c=c):
                 bit = mask[c, b]
                 table[c, b] = jnp.where(bit == 1, count, cap)
                 return count + bit
 
             total = lax.fori_loop(0, n_blocks, fill, total)
 
-    for i in range(2):
-        local[i].wait()
-        remote[i].wait_recv()
+    small[0].wait()
+    number(in_mask, slots_in)
 
     def lanes(i):
         return pl.ds(pl.multiple_of(i * pair, pair), pair)
@@ -224,42 +223,56 @@
         to = z - 1 + 2 * less(src, z, n_z)
         return passed(at(src, x) * pieces + p, feat_z_send.at[src, p], dev(at(to, x)))
 
-    peer_last = at(z, 1 - x) * pieces + last
-
-    def forward_peer(k):
-        return passed(peer_last, peer_send.at[k], (below, above)[k])
+    def forward_peer(k, p):
+        part = at(z, 1 - x) * pieces + p
+        return passed(part, peer_send.at[k, p - straight], (below, above)[k])
 
     def goes_on(src):
         return ((src < z) & has_above) | ((src > z) & has_below)
 
     def by_x(other, p):
         near = (other == z - 1) | (other == z + 1)
-        return jnp.logical_not(near & (p == last))
+        return jnp.logical_not(near & (p >= straight))
+
+    def take(src, p):
+        arrived(at(src, x) * pieces + p)
+        when(goes_on(src), lambda: forward_z(src, p).start())
+        when(by_x(src, p), lambda: forward_x(src, p).start())
 
     for p in range(pieces):
-        own[p].wait()
+        when(has_below, lambda: take(z - 1, p))
+        when(has_above, lambda: take(z + 1, p))
+        arrived(at(z, 1 - x) * pieces + p)
+        if p >= straight:
+            when(has_below, lambda: forward_peer(0, p).start())
+            when(has_above, lambda: forward_peer(1, p).start())
+
+    for i in range(2):
+        local[i].wait()
+        remote[i].wait_recv()
+    def near_products(p, carry):
         project(t * pieces + p)
-    for p in range(pieces):
-        arrived(at(z, 1 - x) * pieces + p)
-        if p == last:
-            when(has_below, lambda: forward_peer(0).start())
-            when(has_above, lambda: forward_peer(1).start())
+        project(at(z, 1 - x) * pieces + p)
+        when(has_below, lambda: project(at(z - 1, x) * pieces + p))
+        when(has_above, lambda: project(at(z + 1, x) * pieces + p))
+        return carry
+
+    lax.fori_loop(0, pieces, near_products, 0)
 
     def gather_step(k, carry):
         j, p = lax.div(k, pieces), lax.rem(k, pieces)
         src = by_distance(z, j, n_z)
-        arrived(at(src, x) * pieces + p)
-        when(goes_on(src), lambda: forward_z(src, p).start())
-        when(by_x(src, p), lambda: forward_x(src, p).start())
-        before = by_distance(z, j - 1, n_z)
-        part = at(before, 1 - x) * pieces + p
-
-        when(j > 1, lambda: arrived(part))
-        project(part)
-        project(at(src, x) * pieces + p)
+        far = jnp.logical_not((src == z - 1) | (src == z + 1))
+        when(far, lambda: take(src, p))
+        before = at(by_distance(z, j - 1, n_z), 1 - x) * pieces + p
+        arrived(before)
+        project(before)
+        when(far, lambda: project(at(src, x) * pieces + p))
         return carry
 
-    lax.fori_loop(pieces, n_z * pieces, gather_step, 0)
+    lax.fori_loop(2 * pieces, n_z * pieces, gather_step, 0)
+    small[1].wait()
+    number(out_mask, slots_out)
     farthest = at(by_distance(z, n_z - 1, n_z), 1 - x) * pieces
     for p in range(pieces):
         arrived(farthest + p)
@@ -290,21 +303,28 @@
     def wide(value):
         return value.astype(jnp.float32)
 
-    def side_to(k):
+    def side_to(k, p):
+        q = p - straight
         return send(
-            side_out.at[k], side_in.at[1 - k], side_send.at[k], side_recv.at[1 - k],
+            side_out.at[k, q], side_in.at[1 - k, q], side_send.at[k, q], side_recv.at[1 - k, q],
             (below, above)[k],
         )
 
-    def side_go(k):
+    def side_from(k, p):
+        q = p - straight
+        send(
+            side_out.at[k, q], side_in.at[k, q], side_send.at[k, q], side_recv.at[k, q], x_peer
+        ).wait_recv()
+
+    def side_go(k, p):
         dst = z - 1 + 2 * k
 
         def store(i):
-            part = at(dst, 1 - x) * pieces + last
-            side_out[k, :, lanes(i)] = down(part, i).astype(side_out.dtype)
+            value = down(at(dst, 1 - x) * pieces + p, i)
+            side_out[k, p - straight, :, lanes(i)] = value.astype(side_out.dtype)
 
         each(store)
-        side_to(k).start()
+        side_to(k, p).start()
 
     def to_x(dst, p):
         return send(
@@ -325,38 +345,33 @@
         when(by_x(dst, p), lambda: go_x(dst, p))
         return carry
 
-    lax.fori_loop(0, pieces, send_x, 0)
-    when(has_below, lambda: side_go(0))
-    when(has_above, lambda: side_go(1))
-    lax.fori_loop(pieces, n_z * pieces - 1, send_x, 0)
-
-    def go_x_last(use_below, use_above):
+    lax.fori_loop(0, 2, send_x, 0)
+    for p in range(straight, pieces):
+        when(has_below, lambda: side_go(0, p))
+        when(has_above, lambda: side_go(1, p))
+    lax.fori_loop(2, n_z * pieces - SIDE, send_x, 0)
+
+    def go_x_last(p, use_below, use_above):
         def store(i):
-            value = down(at(z, 1 - x) * pieces + last, i)
+            value = down(at(z, 1 - x) * pieces + p, i)
             if use_below:
-                value += wide(side_in[0, :, lanes(i)])
+                value += wide(side_in[0, p - straight, :, lanes(i)])
             if use_above:
-                value += wide(side_in[1, :, lanes(i)])
-            x_out[z, last, :, lanes(i)] = value.astype(x_out.dtype)
+                value += wide(side_in[1, p - straight, :, lanes(i)])
+            x_out[z, p, :, lanes(i)] = value.astype(x_out.dtype)
 
         if use_below:
-            side_from(0)
+            side_from(0, p)
         if use_above:
-            side_from(1)
+            side_from(1, p)
         each(store)
-        to_x(z, last).start()
-
-    def side_from(k):
-        send(
-            side_out.at[k], side_in.at[k], side_send.at[k], side_recv.at[k], x_peer
-        ).wait_recv()
+        to_x(z, p).start()
 
     def by_place(act):
         when(has_below & has_above, lambda: act(True, True))
         when(z == 0, lambda: act(False, True))
         when(z == n_z - 1, lambda: act(True, False))
 
-    by_place(go_x_last)
 
     def to_z(dst, p):
         up = less(z, dst, n_z)
@@ -399,7 +414,10 @@
         to_z(dst, p).start()
         return carry
 
-    lax.fori_loop(0, (n_z - 1) * pieces, pass_on, 0)
+    lax.fori_loop(0, pieces, pass_on, 0)
+    for p in range(straight, pieces):
+        by_place(functools.partial(go_x_last, p))
+    lax.fori_loop(pieces, (n_z - 1) * pieces, pass_on, 0)
 
     mine = pl.ds(pl.multiple_of(s * rows, rows), rows)
 
@@ -423,6 +441,7 @@
             from_z(z, 1, p)
         each(store)
 
+    small[2].wait()
     tokens_all = owner.shape[1]
     flags = (owner[...] == s).astype(jnp.float32)
     first = lax.broadcasted_iota(jnp.int32, (tokens_all, tokens_all), 0)
@@ -455,8 +474,9 @@
         when(has_above, lambda: own_to(p, 2).wait_send())
         to_x(z, p).wait_send()
     for k, there in enumerate((has_below, has_above)):
-        when(there, lambda: forward_peer(k).wait_send())
-        when(there, lambda: side_to(k).wait_send())
+        for p in range(straight, pieces):
+            when(there, lambda: forward_peer(k, p).wait_send())
+            when(there, lambda: side_to(k, p).wait_send())
     for copy in remote:
         copy.wait_send()
 
@@ -502,8 +522,8 @@
             pltpu.VMEM((n_z, pieces, rows, span), kind),
             pltpu.VMEM((n_z, pieces, rows, span), kind),
             pltpu.VMEM((n_z, 2, pieces, rows, span), kind),
-            pltpu.VMEM((2, rows, span), kind),
-            pltpu.VMEM((2, rows, span), kind),
+            pltpu.VMEM((2, SIDE, rows, span), kind),
+            pltpu.VMEM((2, SIDE, rows, span), kind),
             pltpu.VMEM((pieces, 2 * rows, span), kind),
             pltpu.SMEM(in_mask.shape, jnp.int32),
             pltpu.SMEM(out_mask.shape, jnp.int32),
@@ -517,13 +537,13 @@
             dma((3, pieces)),
             dma((n_z, pieces)),
             dma((n_z, pieces)),
-            dma((2,)),
+            dma((2, SIDE)),
             dma((n_z, pieces)),
             dma((n_z, pieces)),
             dma((n_z, pieces)),
             dma((n_z, 2, pieces)),
-            dma((2,)),
-            dma((2,)),
+            dma((2, SIDE)),
+            dma((2, SIDE)),
             dma((pieces,)),
             dma((pieces,)),
         ],

time: 62.4 us -> 61.1 us (0.979)
  Pallas kernels: 60.5 us -> 59.1 us
    pallas_call x1, Pallas kernels: 60.5 us -> 59.1 us  [fused(): pl.pallas_call(functools.partial(kernel, n_z, pieces), out_shape=jax.Shap...]
where the time goes in v3:
time: 61.1 us; the launch traced here: 60.9 us
  Pallas kernels  59.1 us (97%)
  local copies, waits for them, and re-layouts  1.77 us (3%)
    pallas_call x1, Pallas kernels, fused(): pl.pallas_call(functools.partial(kernel, n_z, pieces), out_shape=jax.Shap...  59.1 us
    unnamed x1, local copies, waits for them, and re-layouts  1.77 us

profile of v3, /device:TPU:1, one launch (start us, length us, event | category | flops | bytes accessed | tf_op | source)
XLA Modules:
  0.0 60.9 jit_solution(16867708153757519903)
XLA Ops:
  0.0 59.1 %shard_map.73 = bf16[192,1024]{1,0:T(8,128)(2,1)} custom-call(bf16[128,1024]{1,0:T(8,128)(2,1)} %tokens.1, bf16[48,128,128]{2,1,0:T(8,128)(2,1)} %gate_tiles.1, bf16[48,128,128]{2,1,0:T(8,128)(2,1)} %up_tiles.1, bf16[48,128,128]{2,1,0:T(8,128)(2,1)} %down_tiles.1, s32[2,64]{1,0:T(2,128)} %in_mask_hbm.1, s32[2,64]{1,0:T(2,128)} %out_mask_hbm.1, s32[1,256]{1,0:T(1,128)} %bitcast.1), custom_call_target="tpu_custom_call" | custom-call | tf_op jit(solution)/shard_map/pallas_call | solution.py:507
  59.1 1.8 %copy.9 = bf16[192,1024]{1,0:T(8,128)(2,1)} copy(bf16[192,1024]{1,0:T(8,128)(2,1)} %shard_map.73) | data formatting | bytes 786432
